TPU v7x, 256 devices: a whole 4x4x8 slice. The times are simulated.
256 devices in a mesh: batch: 64 (over y, x, z_hi), chan: 4 (over z_lo, core).
Axes of the slice: x: 4, y: 4, z: 8 (z_hi: 4, z_lo: 2; z = z_hi * 2 + z_lo), core: 2. Of those that a mesh axis runs over, the one named last changes fastest.
Arguments:
- fine_inputs: bfloat16 [64, 32, 32, 512], P('batch'), may hold values from -6 to 6
- fine_upstream: bfloat16 [64, 32, 32, 512], P('batch', None, None, 'chan'), may hold values from -6 to 6
- fine_bank: bfloat16 [8, 9, 512, 512], P(None, None, 'batch', 'chan'), may hold values from -0.09375 to 0.09375
- fine_coefs: float32 [64, 8], replicated, may hold values from 0 to 1, as said below
- coarse_inputs: bfloat16 [64, 16, 16, 512], P('batch'), may hold values from -6 to 6
- coarse_upstream: bfloat16 [64, 16, 16, 512], P('batch', None, None, 'chan'), may hold values from -6 to 6
- coarse_bank: bfloat16 [8, 9, 512, 512], P(None, None, 'batch', 'chan'), may hold values from -0.09375 to 0.09375
- coarse_coefs: float32 [64, 8], replicated, may hold values from 0 to 1, as said below
Outputs:
- fine_delta: bfloat16 [64, 32, 32, 512], P('batch', None, None, 'chan')
- fine_update: float32 [8, 9, 512, 512], P(None, None, 'batch', 'chan')
- fine_logit: float32 [64, 8], P('batch')
- coarse_delta: bfloat16 [64, 16, 16, 512], P('batch', None, None, 'chan')
- coarse_update: float32 [8, 9, 512, 512], P(None, None, 'batch', 'chan')
- coarse_logit: float32 [64, 8], P('batch')
Inputs may be any that keep to these rules, and one draw needn't show every extreme that they name: Each row of fine_coefs is a softmax: positive entries that sum to one. Each row of coarse_coefs is a softmax: positive entries that sum to one.
All inputs are finite; a program needn't handle non-finite values.
Results may differ from a plain program's by a relative error of at most 0.01.
Values may be sent and summed in bfloat16 or wider, within the bound.
A program may use at most 128 MiB of HBM per device.

v0:
```python
import jax
import jax.numpy as jnp
from jax import lax
from jax.sharding import PartitionSpec as P

BANKS = 8
FINE_SIDE = 32
COARSE_SIDE = 16
HIGH = lax.Precision.HIGHEST


def shifted(padded, row_shift, col_shift, side):
    window = padded[:, row_shift : row_shift + side, col_shift : col_shift + side, :]
    return window.reshape(window.shape[0], side * side, window.shape[3])


def local_grads(inputs, upstream, kernels, side):
    samples_here = inputs.shape[0]
    pad_in = jnp.pad(inputs, ((0, 0), (1, 1), (1, 1), (0, 0)))
    pad_up = jnp.pad(upstream, ((0, 0), (1, 1), (1, 1), (0, 0)))
    flat_up = upstream.reshape(samples_here, side * side, upstream.shape[3])
    delta = jnp.zeros((samples_here, side * side, inputs.shape[3]), jnp.float32)
    grad_taps = []
    for row_shift in range(3):
        for col_shift in range(3):
            tap = 3 * row_shift + col_shift
            window_in = shifted(pad_in, row_shift, col_shift, side)
            window_up = shifted(pad_up, 2 - row_shift, 2 - col_shift, side)
            grad_taps.append(
                jnp.einsum("bpc,bpo->bco", window_in, flat_up, preferred_element_type=jnp.float32)
                / side
            )
            delta = delta + jnp.einsum(
                "bpo,bco->bpc", window_up, kernels[:, tap], preferred_element_type=jnp.float32
            )
    return (delta.reshape(samples_here, side, side, inputs.shape[3]), jnp.stack(grad_taps, axis=1))


def one_layer(inputs, upstream, bank_part, coefs, side):
    samples_here = inputs.shape[0]
    first_row = lax.axis_index("batch") * samples_here
    own_coefs = lax.dynamic_slice_in_dim(coefs, first_row, samples_here, 0)
    flat_bank = bank_part.reshape(BANKS, -1).astype(jnp.float32)
    bank_rows = lax.all_gather(bank_part, "batch", axis=2, tiled=True)
    flat_rows = bank_rows.reshape(bank_rows.shape[0], -1).astype(jnp.float32)
    mixed = jnp.dot(own_coefs, flat_rows, precision=HIGH)
    kernels = mixed.reshape((samples_here,) + bank_rows.shape[1:]).astype(jnp.bfloat16)
    delta, kernel_grad = local_grads(inputs, upstream, kernels, side)
    delta_total = lax.psum(delta.astype(jnp.bfloat16), "chan").astype(jnp.float32)
    width = delta.shape[3] // lax.axis_size("chan")
    delta_part = lax.dynamic_slice_in_dim(delta_total, lax.axis_index("chan") * width, width, 3)
    moved = lax.all_to_all(
        kernel_grad.astype(jnp.bfloat16), "batch", split_axis=2, concat_axis=0, tiled=True
    ).astype(kernel_grad.dtype)
    flat_grads = moved.reshape(moved.shape[0], -1)
    update = jnp.dot(coefs.T, flat_grads, precision=HIGH).reshape(bank_part.shape)
    dcoef_part = lax.dot_general(flat_grads, flat_bank, (((1,), (1,)), ((), ())), precision=HIGH)
    return (delta_part.astype(jnp.bfloat16), update, dcoef_part)


def logit_grads(coefs, totals, samples_here):
    first_row = lax.axis_index("batch") * samples_here
    own_coefs = lax.dynamic_slice_in_dim(coefs, first_row, samples_here, 0)
    own_totals = lax.dynamic_slice_in_dim(totals, first_row, samples_here, 0)
    return own_coefs * (own_totals - jnp.sum(own_coefs * own_totals, axis=1, keepdims=True))


def per_device(
    fine_inputs,
    fine_upstream,
    fine_bank,
    fine_coefs,
    coarse_inputs,
    coarse_upstream,
    coarse_bank,
    coarse_coefs,
):
    fine_delta, fine_update, fine_partial = one_layer(
        fine_inputs, fine_upstream, fine_bank, fine_coefs, FINE_SIDE
    )
    coarse_delta, coarse_update, coarse_partial = one_layer(
        coarse_inputs, coarse_upstream, coarse_bank, coarse_coefs, COARSE_SIDE
    )
    fine_total, coarse_total = lax.psum((fine_partial, coarse_partial), ("batch", "chan"))
    samples_here = fine_inputs.shape[0]
    fine_logit = logit_grads(fine_coefs, fine_total, samples_here)
    coarse_logit = logit_grads(coarse_coefs, coarse_total, samples_here)
    return (fine_delta, fine_update, fine_logit, coarse_delta, coarse_update, coarse_logit)


def solution(mesh):
    return jax.shard_map(
        per_device,
        mesh=mesh,
        in_specs=(
            P("batch", None, None, None),
            P("batch", None, None, "chan"),
            P(None, None, "batch", "chan"),
            P(),
            P("batch", None, None, None),
            P("batch", None, None, "chan"),
            P(None, None, "batch", "chan"),
            P(),
        ),
        out_specs=(
            P("batch", None, None, "chan"),
            P(None, None, "batch", "chan"),
            P("batch", None),
            P("batch", None, None, "chan"),
            P(None, None, "batch", "chan"),
            P("batch", None),
        ),
        check_vma=False,
    )
```

profile of v0, /device:TPU:1, one launch (start us, length us, event | category | flops | bytes accessed | tf_op | source)
XLA Modules:
  0.0 524.2 jit_solution(8585332356747162847)
XLA Ops:
  7.2 0.7 all-gather.5.cloned.1.call-update
  8.0 0.7 all-gather.3.cloned.1.call-update
  8.7 1.2 fusion.60
  12.3 2.2 copy.31
  14.5 15.2 %all-to-all-start.1 = ((bf16[1,9,512,128]{3,1,0,2:T(8,128)(2,1)}), bf16[1,9,512,128]{3,1,0,2:T(8,128)(2,1)S(1)}, u32[]{:S(2)}, u32[]{:S(2)}) async-start(bf16[1,9,512,128]{3,1,0,2:T(8,128)(2,1)} %copy.31), calls=%async_computation.1 | async-start | bytes 4194304 | tf_op jit(solution)/shard_map/all_to_all | solution.py:52
  29.8 0.5 fusion.78
  30.3 0.5 fusion.76
  30.8 0.5 fusion.74
  31.4 0.5 fusion.72
  31.9 0.5 fusion.70
  32.5 0.5 fusion.68
  33.0 0.6 fusion.66
  33.6 0.5 fusion.64
  34.1 0.5 fusion.62
  34.7 2.2 copy.28
  36.9 51.0 %all-to-all-done.1 = bf16[1,9,512,128]{3,1,0,2:T(8,128)(2,1)S(1)} async-done(((bf16[1,9,512,128]{3,1,0,2:T(8,128)(2,1)}), bf16[1,9,512,128]{3,1,0,2:T(8,128)(2,1)S(1)}, u32[]{:S(2)}, u32[]{:S(2)}) %all-to-all-start.1) | async-done | bytes 1179680 | tf_op jit(solution)/shard_map/all_to_all | solution.py:52
  87.9 5.9 %all-to-all-start = ((bf16[1,9,512,128]{3,1,0,2:T(8,128)(2,1)}), bf16[1,9,512,128]{3,1,0,2:T(8,128)(2,1)}, u32[]{:S(2)}, u32[]{:S(2)}) async-start(bf16[1,9,512,128]{3,1,0,2:T(8,128)(2,1)} %copy.28), calls=%async_computation | async-start | bytes 4194304 | tf_op jit(solution)/shard_map/all_to_all | solution.py:52
  94.1 0.6 copy.41
  94.7 0.6 copy.40
  95.3 0.8 pad_slice_fusion.24
  96.1 1.3 pad_slice_fusion.16
  97.8 1.3 reshape.891
  99.1 48.8 %all-to-all-done = bf16[1,9,512,128]{3,1,0,2:T(8,128)(2,1)} async-done(((bf16[1,9,512,128]{3,1,0,2:T(8,128)(2,1)}), bf16[1,9,512,128]{3,1,0,2:T(8,128)(2,1)}, u32[]{:S(2)}, u32[]{:S(2)}) %all-to-all-start) | async-done | bytes 1179680 | tf_op jit(solution)/shard_map/all_to_all | solution.py:52
  148.0 2.0 copy.61
  150.0 0.5 reshape.858
  150.5 0.6 fusion.166
  151.1 80.3 %all-gather.5.cloned.1.call-done = bf16[8,9,512,128]{3,2,1,0:T(8,128)(2,1)} async-done(((bf16[8,9,8,128]{3,2,1,0:T(8,128)(2,1)}), bf16[8,9,512,128]{3,2,1,0:T(8,128)(2,1)}) %all-gather.5.cloned.1.call-update) | async-done | bytes 9437200 | tf_op jit(solution)/shard_map/all_gather | solution.py:44
  231.4 16.2 %copy.58 = bf16[1,8,4608,128]{3,1,2,0:T(8,128)(2,1)S(1)} copy(bf16[1,8,4608,128]{3,2,1,0:T(8,128)(2,1)} %bitcast.537) | data formatting | bytes 18874368
  247.6 8.0 %fusion.146 = f32[1,9,512,128]{3,0,2,1:T(1,128)S(1)} fusion(bf16[9,512,128,8]{2,3,1,0:T(8,128)(2,1)S(1)} %bitcast.532, f32[1,8]{0,1:T(8,128)S(1)} %get-tuple-element.44), kind=kOutput, calls=%fused_computation.215 | convolution fusion | flops 56623104 | bytes 11796512 | tf_op jit(solution)/shard_map/dot_general | solution.py:46
  255.8 136.1 %all-gather.3.cloned.1.call-done = bf16[8,9,512,128]{3,2,1,0:T(8,128)(2,1)} async-done(((bf16[8,9,8,128]{3,2,1,0:T(8,128)(2,1)}), bf16[8,9,512,128]{3,2,1,0:T(8,128)(2,1)}) %all-gather.3.cloned.1.call-update) | async-done | bytes 9437200 | tf_op jit(solution)/shard_map/all_gather | solution.py:44
  391.9 16.2 %copy.59 = bf16[1,8,4608,128]{3,1,2,0:T(8,128)(2,1)S(1)} copy(bf16[1,8,4608,128]{3,2,1,0:T(8,128)(2,1)} %bitcast.536) | data formatting | bytes 18874368
  408.1 8.3 %fusion.148 = f32[1,9,512,128]{3,0,2,1:T(1,128)S(1)} fusion(bf16[9,512,128,8]{2,3,1,0:T(8,128)(2,1)S(1)} %bitcast.533, f32[1,8]{0,1:T(8,128)S(1)} %get-tuple-element.45), kind=kOutput, calls=%fused_computation.217 | convolution fusion | flops 56623104 | bytes 11796512 | tf_op jit(solution)/shard_map/dot_general | solution.py:46
  416.6 0.8 copy-done.9
  417.3 0.4 fusion.130
  417.8 0.5 copy-done.8
  418.3 0.4 fusion.131
  418.7 0.5 copy-done.7
  419.2 0.4 fusion.133
  419.7 0.5 copy-done.6
  420.2 0.4 fusion.134
  420.6 0.5 copy-done.5
  421.1 0.4 fusion.135
  421.6 0.5 copy-done.4
  422.1 0.4 fusion.136
  422.5 0.5 copy-done.3
  423.0 0.4 fusion.129
  423.5 0.5 copy-done.2
  424.0 0.4 fusion.132
  424.4 0.4 copy-done.18
  427.9 0.9 fusion.6
  428.8 1.9 fusion.4
  430.7 1.2 copy-done
  432.0 0.6 fusion.167
  432.5 0.8 copy.33
  433.3 0.8 copy.34
  434.1 0.4 fusion.122
  434.6 0.4 fusion.125
  435.0 76.0 %all-reduce.4 = (f32[64,8]{1,0:T(8,128)S(1)}, f32[64,8]{1,0:T(8,128)S(1)}) all-reduce(f32[64,8]{1,0:T(8,128)S(1)} %fusion.125, f32[64,8]{1,0:T(8,128)S(1)} %fusion.122), channel_id=1, replica_groups=mesh['batch'=64,'chan'=4] {'batch','chan'}, use_global_device_ids=true, to_apply=%region_1.2 | all-reduce | flops 1024 | bytes 8192 | tf_op jit(solution)/shard_map/psum | solution.py:84
  511.0 0.6 multiply_reduce_fusion
  511.6 0.6 multiply_reduce_fusion.1
  512.2 1.2 subtract_multiply_fusion
  513.3 1.2 subtract_multiply_fusion.1
  514.5 1.7 convert_convert_fusion
  516.2 1.5 convert_convert_fusion.1
  (71 shorter events, 6.4 us)
Async XLA Ops:
  7.2 2.8 copy-start.10
  7.2 2.7 copy-start.27
  7.2 224.2 %all-gather.5.cloned.1.call-start = ((), (), s32[]{:S(2)}) async-start(), calls=%async_computation.3 | async-start | bytes 9584640 | tf_op jit(solution)/shard_map/all_gather | solution.py:44
  7.9 384.0 %all-gather.3.cloned.1.call-start = ((), (), s32[]{:S(2)}) async-start(), calls=%async_computation.2 | async-start | bytes 9584640 | tf_op jit(solution)/shard_map/all_gather | solution.py:44
  14.5 15.3 %copy-start.1 = (bf16[1,32,32,128]{3,2,1,0:T(8,128)(2,1)S(1)}, bf16[1,32,32,128]{3,2,1,0:T(8,128)(2,1)}, u32[]{:S(2)}) copy-start(bf16[1,32,32,128]{3,2,1,0:T(8,128)(2,1)} %param.9) | copy-start | bytes 786436
  14.5 15.3 %copy-start.26 = (bf16[1,32,32,512]{3,2,1,0:T(8,128)(2,1)S(1)}, bf16[1,32,32,512]{3,2,1,0:T(8,128)(2,1)}, u32[]{:S(2)}) copy-start(bf16[1,32,32,512]{3,2,1,0:T(8,128)(2,1)} %param.8) | copy-start | bytes 3145732
  14.5 73.4 %all-to-all-start.1 = ((bf16[1,9,512,128]{3,1,0,2:T(8,128)(2,1)}), bf16[1,9,512,128]{3,1,0,2:T(8,128)(2,1)S(1)}, u32[]{:S(2)}, u32[]{:S(2)}) async-start(bf16[1,9,512,128]{3,1,0,2:T(8,128)(2,1)} %copy.31), calls=%async_computation.1 | async-start | bytes 4194304 | tf_op jit(solution)/shard_map/all_to_all | solution.py:52
  36.9 57.2 %copy-start.22 = (f32[64,8]{0,1:T(8,128)S(1)}, f32[64,8]{0,1:T(8,128)}, u32[]{:S(2)}) copy-start(f32[64,8]{0,1:T(8,128)} %param.11) | copy-start | bytes 6148
  36.9 57.2 %copy-start.23 = (f32[64,8]{0,1:T(8,128)S(1)}, f32[64,8]{0,1:T(8,128)}, u32[]{:S(2)}) copy-start(f32[64,8]{0,1:T(8,128)} %param.15) | copy-start | bytes 6148
  87.9 60.1 %all-to-all-start = ((bf16[1,9,512,128]{3,1,0,2:T(8,128)(2,1)}), bf16[1,9,512,128]{3,1,0,2:T(8,128)(2,1)}, u32[]{:S(2)}, u32[]{:S(2)}) async-start(bf16[1,9,512,128]{3,1,0,2:T(8,128)(2,1)} %copy.28), calls=%async_computation | async-start | bytes 4194304 | tf_op jit(solution)/shard_map/all_to_all | solution.py:52
  93.8 420.7 %all-reduce.8.cloned.1.call-start = ((), (), s32[]{:S(2)}) async-start(), calls=%async_computation.4 | async-start | bytes 2621440 | tf_op jit(solution)/shard_map/psum | solution.py:49
  416.4 1.0 copy-start.9
  417.3 0.9 copy-start.8
  418.3 0.9 copy-start.7
  419.2 0.9 copy-start.6
  420.2 0.9 copy-start.5
  421.1 0.9 copy-start.4
  422.1 0.9 copy-start.3
  423.0 0.9 copy-start.2
  424.0 0.8 copy-start.18
  424.0 1.1 copy-start.17
  424.4 0.9 copy-start.16
  425.1 0.8 copy-start.15
  425.3 0.8 copy-start.11
  425.9 0.8 copy-start.14
  426.2 0.8 copy-start.13
  426.8 0.8 copy-start.12
  427.0 0.8 copy-start.19
  430.7 1.3 copy-start
  431.9 2.1 copy-start.20
  433.3 1.2 copy-start.21
  434.5 76.4 %copy-start.25 = (f32[1,8]{1,0:T(1,128)S(1)}, f32[1,8]{1,0:T(1,128)}, u32[]{:S(2)}) copy-start(f32[1,8]{1,0:T(1,128)} %copy.41) | copy-start | bytes 100
  434.5 77.0 %copy-start.24 = (f32[1,8]{1,0:T(1,128)S(1)}, f32[1,8]{1,0:T(1,128)}, u32[]{:S(2)}) copy-start(f32[1,8]{1,0:T(1,128)} %copy.40) | copy-start | bytes 100
Sparse Core Ops, SparseCore 0:
  11.1 220.1 all-gather.4
  234.5 157.3 all-gather.2
  430.8 49.6 all-reduce.7
where the time goes:
time: 525 us; the launch traced here: 524 us
  waiting for transfers between devices  318 us (61%)
  blocking collectives  76 us (14%)
  local copies, waits for them, and re-layouts  53.3 us (10%)
  matrix products  34.7 us (7%)
  starting transfers between devices  21.4 us (4%)
  between operations  14.2 us (3%)
  other arithmetic  7.02 us (1%)
    all_gather x2, waiting for transfers between devices, one_layer(): bank_rows = lax.all_gather(bank_part, 'batch', axis=2, tiled=True)  216 us
    all_to_all x2, waiting for transfers between devices, one_layer(): lax.all_to_all(kernel_grad.astype(jnp.bfloat16), 'batch', split_axis=2, c...  99.9 us
    psum x1, blocking collectives, per_device(): lax.psum((fine_partial, coarse_partial), ('batch', 'chan'))  76 us
    unnamed x62, local copies, waits for them, and re-layouts  42.3 us
    all_to_all x2, starting transfers between devices, one_layer(): lax.all_to_all(kernel_grad.astype(jnp.bfloat16), 'batch', split_axis=2, c...  21.1 us
    dot_general x2, matrix products, one_layer(): mixed = jnp.dot(own_coefs, flat_rows, precision=HIGH)  16.3 us
  transfers between devices with their start and end apart: 5, of which 4 were waited for; matrix products, arithmetic and copies ran while one was open for 10% of the time, Pallas kernels for 0%

commit v1 on v0

--- a/solution.py
+++ b/solution.py
@@ -49,8 +49,14 @@
     delta_total = lax.psum(delta.astype(jnp.bfloat16), "chan").astype(jnp.float32)
     width = delta.shape[3] // lax.axis_size("chan")
     delta_part = lax.dynamic_slice_in_dim(delta_total, lax.axis_index("chan") * width, width, 3)
-    moved = lax.all_to_all(
-        kernel_grad.astype(jnp.bfloat16), "batch", split_axis=2, concat_axis=0, tiled=True
+    moved = jnp.concatenate(
+        lax.all_to_all(
+            jnp.stack(jnp.split(kernel_grad.astype(jnp.bfloat16), lax.axis_size("batch"), axis=2)),
+            "batch",
+            0,
+            0,
+        ),
+        axis=0,
     ).astype(kernel_grad.dtype)
     flat_grads = moved.reshape(moved.shape[0], -1)
     update = jnp.dot(coefs.T, flat_grads, precision=HIGH).reshape(bank_part.shape)

time: 525 us -> 506 us (0.964)
  waiting for transfers between devices: 318 us -> 224 us
  local copies, waits for them, and re-layouts: 53.3 us -> 121 us
  starting transfers between devices: 21.4 us -> 27.5 us
    all_to_all x2, waiting for transfers between devices: 99.9 us -> 0.01 us  [one_layer(): lax.all_to_all(jnp.stack(jnp.split(kernel_grad.astype(jnp.bfloat16), lax....]
    unnamed x62 -> x186, local copies, waits for them, and re-layouts: 42.3 us -> 118 us
    all_to_all x2, starting transfers between devices: 21.1 us -> 27.4 us  [one_layer(): lax.all_to_all(jnp.stack(jnp.split(kernel_grad.astype(jnp.bfloat16), lax....]
    all_gather x2, waiting for transfers between devices: 216 us -> 222 us  [one_layer(): bank_rows = lax.all_gather(bank_part, 'batch', axis=2, tiled=True)]
  transfers between devices with their start and end apart: 5 -> 5, of which waited for: 4 -> 2; matrix products, arithmetic and copies ran while one was open for 10% -> 30% of each run, Pallas kernels for 0% -> 0%
where the time goes in v1:
time: 506 us; the launch traced here: 505 us
  waiting for transfers between devices  224 us (44%)
  local copies, waits for them, and re-layouts  121 us (24%)
  blocking collectives  75.9 us (15%)
  matrix products  35.6 us (7%)
  starting transfers between devices  27.5 us (5%)
  between operations  14.3 us (3%)
  other arithmetic  7.02 us (1%)
    all_gather x2, waiting for transfers between devices, one_layer(): bank_rows = lax.all_gather(bank_part, 'batch', axis=2, tiled=True)  222 us
    unnamed x186, local copies, waits for them, and re-layouts  118 us
    psum x1, blocking collectives, per_device(): lax.psum((fine_partial, coarse_partial), ('batch', 'chan'))  75.9 us
    all_to_all x2, starting transfers between devices, one_layer(): lax.all_to_all(jnp.stack(jnp.split(kernel_grad.astype(jnp.bfloat16), lax....  27.4 us
    dot_general x2, matrix products, one_layer(): mixed = jnp.dot(own_coefs, flat_rows, precision=HIGH)  16.3 us
  transfers between devices with their start and end apart: 5, of which 2 were waited for; matrix products, arithmetic and copies ran while one was open for 30% of the time, Pallas kernels for 0%

profile of v1, /device:TPU:1, one launch (start us, length us, event | category | flops | bytes accessed | tf_op | source)
XLA Modules:
  0.0 505.0 jit_solution(9787268613415035324)
XLA Ops:
  7.2 0.7 all-gather.5.cloned.1.call-update
  8.0 0.7 all-gather.3.cloned.1.call-update
  8.7 1.2 fusion.68
  14.2 0.6 constant_dynamic-update-slice_fusion.124
  14.8 0.6 constant_dynamic-update-slice_fusion.123
  18.4 0.6 constant_dynamic-update-slice_fusion.117
  22.7 0.6 constant_dynamic-update-slice_fusion.110
  24.5 0.6 constant_dynamic-update-slice_fusion.107
  26.9 0.6 constant_dynamic-update-slice_fusion.103
  30.5 0.6 constant_dynamic-update-slice_fusion.97
  31.2 0.6 constant_dynamic-update-slice_fusion.96
  31.8 0.6 constant_dynamic-update-slice_fusion.95
  38.4 0.6 constant_dynamic-update-slice_fusion.84
  43.9 0.6 constant_dynamic-update-slice_fusion.75
  44.5 0.6 constant_dynamic-update-slice_fusion.74
  49.3 0.6 constant_dynamic-update-slice_fusion.66
  50.5 0.6 constant_dynamic-update-slice_fusion.64
  51.1 15.2 %all-to-all-start.1 = ((bf16[64,1,9,8,128]{4,3,2,1,0:T(8,128)(2,1)}), bf16[64,1,9,8,128]{4,3,2,1,0:T(8,128)(2,1)S(1)}, u32[]{:S(2)}, u32[]{:S(2)}) async-start(bf16[64,1,9,8,128]{4,3,2,1,0:T(8,128)(2,1)} %constant_dynamic-update-slice_fusion.64), calls=%async_computation.1 | async-start | bytes 2359296 | tf_op jit(solution)/shard_map/all_to_all | solution.py:53
  66.7 1.4 pad_slice_fusion.16
  73.5 0.6 constant_dynamic-update-slice_fusion.63
  75.3 0.6 constant_dynamic-update-slice_fusion.60
  77.2 0.6 constant_dynamic-update-slice_fusion.57
  78.4 0.6 constant_dynamic-update-slice_fusion.55
  79.0 0.6 constant_dynamic-update-slice_fusion.54
  80.2 0.6 constant_dynamic-update-slice_fusion.52
  80.8 0.6 constant_dynamic-update-slice_fusion.51
  81.4 0.6 constant_dynamic-update-slice_fusion.50
  83.9 0.6 constant_dynamic-update-slice_fusion.46
  85.7 0.6 constant_dynamic-update-slice_fusion.43
  86.3 0.6 constant_dynamic-update-slice_fusion.42
  86.9 0.6 constant_dynamic-update-slice_fusion.41
  89.3 0.6 constant_dynamic-update-slice_fusion.37
  89.9 0.6 constant_dynamic-update-slice_fusion.36
  90.5 0.6 constant_dynamic-update-slice_fusion.35
  91.1 0.6 constant_dynamic-update-slice_fusion.34
  95.4 0.6 constant_dynamic-update-slice_fusion.27
  97.2 0.6 constant_dynamic-update-slice_fusion.24
  99.0 0.6 constant_dynamic-update-slice_fusion.21
  100.8 0.6 constant_dynamic-update-slice_fusion.18
  101.4 0.6 constant_dynamic-update-slice_fusion.17
  102.7 0.6 constant_dynamic-update-slice_fusion.15
  106.3 0.8 pad_slice_fusion.24
  107.1 0.6 constant_dynamic-update-slice_fusion.9
  108.9 0.6 constant_dynamic-update-slice_fusion.6
  111.3 0.6 constant_dynamic-update-slice_fusion.2
  112.5 0.6 constant_dynamic-update-slice_fusion
  113.2 12.2 %all-to-all-start = ((bf16[64,1,9,8,128]{4,3,2,1,0:T(8,128)(2,1)}), bf16[64,1,9,8,128]{4,3,2,1,0:T(8,128)(2,1)S(1)}, u32[]{:S(2)}, u32[]{:S(2)}) async-start(bf16[64,1,9,8,128]{4,3,2,1,0:T(8,128)(2,1)} %constant_dynamic-update-slice_fusion), calls=%async_computation | async-start | bytes 2359296 | tf_op jit(solution)/shard_map/all_to_all | solution.py:53
  125.4 1.3 fusion.9
  126.7 87.5 %all-gather.5.cloned.1.call-done = bf16[8,9,512,128]{3,2,1,0:T(8,128)(2,1)} async-done(((bf16[8,9,8,128]{3,2,1,0:T(8,128)(2,1)}), bf16[8,9,512,128]{3,2,1,0:T(8,128)(2,1)}) %all-gather.5.cloned.1.call-update) | async-done | bytes 9437200 | tf_op jit(solution)/shard_map/all_gather | solution.py:44
  214.2 16.2 %copy.58 = bf16[1,8,4608,128]{3,1,2,0:T(8,128)(2,1)S(1)} copy(bf16[1,8,4608,128]{3,2,1,0:T(8,128)(2,1)} %bitcast.1043) | data formatting | bytes 18874368
  230.4 8.0 %fusion.156 = f32[1,9,512,128]{3,0,2,1:T(1,128)S(1)} fusion(bf16[9,512,128,8]{2,3,1,0:T(8,128)(2,1)S(1)} %bitcast.1038, f32[1,8]{0,1:T(8,128)S(1)} %get-tuple-element.32), kind=kOutput, calls=%fused_computation.479 | convolution fusion | flops 56623104 | bytes 11796512 | tf_op jit(solution)/shard_map/dot_general | solution.py:46
  238.7 134.7 %all-gather.3.cloned.1.call-done = bf16[8,9,512,128]{3,2,1,0:T(8,128)(2,1)} async-done(((bf16[8,9,8,128]{3,2,1,0:T(8,128)(2,1)}), bf16[8,9,512,128]{3,2,1,0:T(8,128)(2,1)}) %all-gather.3.cloned.1.call-update) | async-done | bytes 9437200 | tf_op jit(solution)/shard_map/all_gather | solution.py:44
  373.3 16.2 %copy.59 = bf16[1,8,4608,128]{3,1,2,0:T(8,128)(2,1)S(1)} copy(bf16[1,8,4608,128]{3,2,1,0:T(8,128)(2,1)} %bitcast.1042) | data formatting | bytes 18874368
  389.6 8.3 %fusion.158 = f32[1,9,512,128]{3,0,2,1:T(1,128)S(1)} fusion(bf16[9,512,128,8]{2,3,1,0:T(8,128)(2,1)S(1)} %bitcast.1039, f32[1,8]{0,1:T(8,128)S(1)} %get-tuple-element.33), kind=kOutput, calls=%fused_computation.481 | convolution fusion | flops 56623104 | bytes 11796512 | tf_op jit(solution)/shard_map/dot_general | solution.py:46
  398.0 0.8 copy-done.10
  404.6 0.9 fusion.6
  410.3 1.9 fusion.4
  413.1 0.8 copy.18
  413.9 0.8 copy.17
  416.0 75.9 %all-reduce.4 = (f32[64,8]{1,0:T(8,128)S(1)}, f32[64,8]{1,0:T(8,128)S(1)}) all-reduce(f32[64,8]{1,0:T(8,128)S(1)} %fusion.11, f32[64,8]{1,0:T(8,128)S(1)} %fusion.7), channel_id=1, replica_groups=mesh['batch'=64,'chan'=4] {'batch','chan'}, use_global_device_ids=true, to_apply=%region_1.2 | all-reduce | flops 1024 | bytes 8192 | tf_op jit(solution)/shard_map/psum | solution.py:90
  493.0 1.2 subtract_multiply_fusion
  494.2 1.2 subtract_multiply_fusion.1
  495.4 1.7 convert_convert_fusion
  497.0 1.5 convert_convert_fusion.1
  (191 shorter events, 75.5 us)
Async XLA Ops:
  7.2 2.8 copy-start.26
  7.2 2.8 copy-start.11
  7.2 207.0 %all-gather.5.cloned.1.call-start = ((), (), s32[]{:S(2)}) async-start(), calls=%async_computation.3 | async-start | bytes 9584640 | tf_op jit(solution)/shard_map/all_gather | solution.py:44
  7.9 365.4 %all-gather.3.cloned.1.call-start = ((), (), s32[]{:S(2)}) async-start(), calls=%async_computation.2 | async-start | bytes 9584640 | tf_op jit(solution)/shard_map/all_gather | solution.py:44
  51.1 15.3 %copy-start.23 = (f32[64,8]{0,1:T(8,128)S(1)}, f32[64,8]{0,1:T(8,128)}, u32[]{:S(2)}) copy-start(f32[64,8]{0,1:T(8,128)} %param.15) | copy-start | bytes 6148
  51.1 15.3 %copy-start.24 = (f32[64,8]{0,1:T(8,128)S(1)}, f32[64,8]{0,1:T(8,128)}, u32[]{:S(2)}) copy-start(f32[64,8]{0,1:T(8,128)} %param.11) | copy-start | bytes 6148
  51.1 15.5 %copy-start.2 = (bf16[1,32,32,128]{3,2,1,0:T(8,128)(2,1)S(1)}, bf16[1,32,32,128]{3,2,1,0:T(8,128)(2,1)}, u32[]{:S(2)}) copy-start(bf16[1,32,32,128]{3,2,1,0:T(8,128)(2,1)} %param.9) | copy-start | bytes 786436
  51.1 62.0 %all-to-all-start.1 = ((bf16[64,1,9,8,128]{4,3,2,1,0:T(8,128)(2,1)}), bf16[64,1,9,8,128]{4,3,2,1,0:T(8,128)(2,1)S(1)}, u32[]{:S(2)}, u32[]{:S(2)}) async-start(bf16[64,1,9,8,128]{4,3,2,1,0:T(8,128)(2,1)} %constant_dynamic-update-slice_fusion.64), calls=%async_computation.1 | async-start | bytes 2359296 | tf_op jit(solution)/shard_map/all_to_all | solution.py:53
  66.6 1.9 copy-start.25
  113.2 299.0 %all-to-all-start = ((bf16[64,1,9,8,128]{4,3,2,1,0:T(8,128)(2,1)}), bf16[64,1,9,8,128]{4,3,2,1,0:T(8,128)(2,1)S(1)}, u32[]{:S(2)}, u32[]{:S(2)}) async-start(bf16[64,1,9,8,128]{4,3,2,1,0:T(8,128)(2,1)} %constant_dynamic-update-slice_fusion), calls=%async_computation | async-start | bytes 2359296 | tf_op jit(solution)/shard_map/all_to_all | solution.py:53
  125.3 370.0 %all-reduce.8.cloned.1.call-start = ((), (), s32[]{:S(2)}) async-start(), calls=%async_computation.4 | async-start | bytes 2621440 | tf_op jit(solution)/shard_map/psum | solution.py:49
  397.8 1.0 copy-start.10
  398.8 0.9 copy-start.9
  399.7 0.9 copy-start.8
  400.7 0.8 copy-start.19
  400.7 1.1 copy-start.18
  401.1 0.9 copy-start.17
  401.8 0.8 copy-start.16
  402.0 0.8 copy-start.12
  402.6 0.8 copy-start.15
  402.9 0.8 copy-start.14
  403.5 0.8 copy-start.13
  403.7 0.8 copy-start.20
  404.0 1.6 copy-start.7
  405.5 1.0 copy-start.6
  406.5 0.9 copy-start.5
  407.4 0.9 copy-start.4
  408.4 0.9 copy-start.3
  409.3 0.9 copy-start.1
  412.1 1.0 copy-start
  412.2 2.5 copy-start.21
  414.6 0.9 copy-start.22
Sparse Core Ops, SparseCore 0:
  11.1 203.0 all-gather.4
  217.3 155.9 all-gather.2
  412.3 49.6 all-reduce.7
